TPU v7x, 32 devices: a whole 2x2x4 slice. The times are simulated.
32 devices in a mesh: vocab: 8 (over z, y), token: 4 (over x, core).
Axes of the slice: x: 2, y: 2, z: 4, core: 2. Of those that a mesh axis runs over, the one named last changes fastest.
Arguments:
- hidden: bfloat16 [4096, 4096], P(('vocab', 'token')), may hold values from -16 to 16
- cand_embed: bfloat16 [1024, 4096], P('vocab'), may hold values from -0.5 to 0.5
- freq_embed: bfloat16 [32, 4096], P('vocab'), may hold values from -0.09375 to 0.09375
- owner_order: int32 [8], replicated, may hold values from 0 to 7, each once
- cand_blocks: int32 [512, 4], P(('vocab', 'token')), may hold values from 0 to 7, all different within a row; in each aligned block of 16 rows (0 to 15, 16 to 31, ...) at most 16 rows name the same one
- group_tokens: int32 [32, 128], P(('vocab', 'token')), may hold values from 0 to 127, each once within a row
- target_slot: int32 [4096], P(('vocab', 'token')), may hold values from 0 to 543
Outputs:
- logits: bfloat16 [4096, 544], P(('vocab', 'token'))
- loss: float32 [4096], P(('vocab', 'token'))
- grad_hidden: bfloat16 [4096, 4096], P(('vocab', 'token'))
- grad_cand: float32 [1024, 4096], P(('vocab', 'token'))
- grad_freq: float32 [32, 4096], P(('vocab', 'token'))
Inputs may be any that keep to these rules, and one draw needn't show every extreme that they name: `cand_blocks`: each row names 4 different blocks. Among the 16 groups of one device no block is named by more than 16 groups, and some device reaches 16. `group_tokens`: each row lists every number below 128 once. `owner_order`: every number below 8 once.
All inputs are finite; a program needn't handle non-finite values.
Results may differ from a plain program's by a relative error of at most 0.0052.
Values may be sent and summed in bfloat16 or wider, within the bound.
A program may use at most 128 MiB of HBM per device.

v0:
```python
import jax
import jax.numpy as jnp
from jax import lax
from jax.sharding import PartitionSpec as P

D = 4096
BW = 128
K = 4
GTOK = 8
PANEL = 4
G_DEV = 16


def per_device(hidden, cand_embed, freq_embed, owner_order, cand_blocks, group_tokens, target_slot):
    owners_count = lax.axis_size("vocab")
    token_total = hidden.shape[0]
    freq_count = owners_count * PANEL
    capacity = 2 * G_DEV * K // owners_count
    slot_count = owners_count * capacity
    requests = G_DEV * K
    listing = group_tokens[0]
    grouped = hidden[listing]
    targets = target_slot[listing]
    panels = lax.all_gather(freq_embed, "vocab", axis=0, tiled=True)
    freq_table = panels.reshape(owners_count, PANEL, D)[owner_order].reshape(freq_count, D)
    owner_of = cand_blocks.reshape(requests)
    owner_hot = (owner_of[:, None] == jnp.arange(owners_count, dtype=jnp.int32)[None, :]).astype(
        jnp.int32
    )
    ranking = jnp.sum(jnp.cumsum(owner_hot, axis=0) * owner_hot, axis=1) - 1
    landing = owner_of * capacity + ranking
    placed = (landing[None, :] == jnp.arange(slot_count, dtype=jnp.int32)[:, None]).astype(
        jnp.int32
    )
    occupied = jnp.sum(placed, axis=1)
    request_of = jnp.sum(placed * jnp.arange(requests, dtype=jnp.int32)[None, :], axis=1)
    group_of = request_of // K
    block_rank = request_of % K
    group_rows = grouped.reshape(G_DEV, GTOK, D)
    slot_mask = occupied.astype(jnp.bfloat16)[:, None, None]
    send_rows = (group_rows[group_of] * slot_mask).reshape(owners_count, capacity, GTOK, D)
    group_targets = targets.reshape(G_DEV, GTOK)
    column = group_targets[group_of] - freq_count - block_rank[:, None] * BW
    inside = (column >= 0) & (column < BW) & (occupied[:, None] > 0)
    send_column = jnp.where(inside, column, -1).reshape(owners_count, capacity, GTOK)
    got_rows, got_column = (
        lax.all_to_all(send_rows, "vocab", split_axis=0, concat_axis=0, tiled=True),
        lax.all_to_all(send_column, "vocab", split_axis=0, concat_axis=0, tiled=True),
    )
    scores_here = jnp.einsum(
        "scqd,wd->scqw", got_rows, cand_embed, preferred_element_type=jnp.float32
    )
    scores_home = lax.all_to_all(scores_here, "vocab", split_axis=0, concat_axis=0, tiled=True)
    returned = scores_home.reshape(slot_count, GTOK, BW)[landing]
    cand_scores = (
        returned.reshape(G_DEV, K, GTOK, BW).transpose(0, 2, 1, 3).reshape(token_total, K * BW)
    )
    freq_scores = jnp.einsum("td,fd->tf", grouped, freq_table, preferred_element_type=jnp.float32)
    all_scores = jnp.concatenate([freq_scores, cand_scores], axis=1)
    row_top = jnp.max(all_scores, axis=1)
    exponentials = jnp.exp(all_scores - row_top[:, None])
    total = jnp.sum(exponentials, axis=1)
    inverse_total = 1.0 / total
    columns = jnp.arange(all_scores.shape[1], dtype=jnp.int32)
    target_hot = (targets[:, None] == columns[None, :]).astype(jnp.float32)
    token_loss = jnp.log(total) + row_top - jnp.sum(target_hot * all_scores, axis=1)
    prob_freq = (
        exponentials[:, :freq_count] * inverse_total[:, None] - target_hot[:, :freq_count]
    ).astype(jnp.bfloat16)
    slot_live = occupied[:, None].astype(jnp.float32)
    send_scale = (inverse_total.reshape(G_DEV, GTOK)[group_of] * slot_live).reshape(
        owners_count, capacity, GTOK
    )
    send_top = (row_top.reshape(G_DEV, GTOK)[group_of] * slot_live).reshape(
        owners_count, capacity, GTOK
    )
    got_scale, got_top = (
        lax.all_to_all(send_scale, "vocab", split_axis=0, concat_axis=0, tiled=True),
        lax.all_to_all(send_top, "vocab", split_axis=0, concat_axis=0, tiled=True),
    )
    word_index = jnp.arange(BW, dtype=jnp.int32)
    is_target = (got_column[..., None] == word_index).astype(jnp.float32)
    prob_here = (
        jnp.exp(scores_here - got_top[..., None]) * got_scale[..., None] - is_target
    ).astype(jnp.bfloat16)
    hidden_part = jnp.einsum(
        "scqw,wd->scqd", prob_here, cand_embed, preferred_element_type=jnp.float32
    ).astype(jnp.bfloat16)
    parts_home = lax.all_to_all(hidden_part, "vocab", split_axis=0, concat_axis=0, tiled=True)
    window = prob_here
    grad_cand = lax.psum_scatter(
        jnp.einsum("scqw,scqd->wd", window, got_rows, preferred_element_type=jnp.float32),
        "token",
        scatter_dimension=0,
        tiled=True,
    )
    part_rows = parts_home.reshape(slot_count, GTOK, D)[landing].reshape(G_DEV, K, GTOK, D)
    freq_part = jnp.dot(prob_freq, freq_table, preferred_element_type=jnp.float32)
    grad_rows = freq_part + jnp.sum(part_rows, axis=1, dtype=jnp.float32).reshape(token_total, D)
    position_of = (
        jnp.zeros((owners_count,), jnp.int32)
        .at[owner_order]
        .set(jnp.arange(owners_count, dtype=jnp.int32))
    )
    embed_columns = (
        position_of[:, None] * PANEL + jnp.arange(PANEL, dtype=jnp.int32)[None, :]
    ).reshape(freq_count)
    prob_embed = prob_freq[:, embed_columns]
    window = prob_embed
    grad_freq = lax.psum_scatter(
        jnp.einsum("tf,td->fd", window, grouped, preferred_element_type=jnp.float32),
        ("vocab", "token"),
        scatter_dimension=0,
        tiled=True,
    )
    undo = (
        jnp.zeros((token_total,), jnp.int32)
        .at[listing]
        .set(jnp.arange(token_total, dtype=jnp.int32))
    )
    logits = all_scores.astype(jnp.bfloat16)[undo]
    loss = token_loss[undo]
    grad_hidden = grad_rows.astype(jnp.bfloat16)[undo]
    return (logits, loss, grad_hidden, grad_cand, grad_freq)


def solution(mesh):
    in_specs = (
        P(("vocab", "token"), None),
        P("vocab", None),
        P("vocab", None),
        P(),
        P(("vocab", "token"), None),
        P(("vocab", "token"), None),
        P(("vocab", "token")),
    )
    out_specs = (
        P(("vocab", "token"), None),
        P(("vocab", "token")),
        P(("vocab", "token"), None),
        P(("vocab", "token"), None),
        P(("vocab", "token"), None),
    )
    return jax.shard_map(
        per_device, mesh=mesh, in_specs=in_specs, out_specs=out_specs, check_vma=False
    )
```

profile of v0, /device:TPU:0, one launch (start us, length us, event | category | flops | bytes accessed | tf_op | source)
XLA Modules:
  0.0 573.3 jit_solution(2524966580494172715)
XLA Ops:
  8.0 0.7 fusion.16
  8.8 0.8 copy.39
  10.2 3.6 gather_fusion
  13.8 6.4 %gather_fusion.2 = bf16[128,8,4096]{2,1,0:T(8,128)(2,1)} fusion(bf16[16,8,4096]{2,1,0:T(8,128)(2,1)S(1)} %bitcast.70, s32[1024]{0:T(1024)S(1)} %pad_clamp_fusion.3), kind=kCustom, calls=%fused_computation.2 | custom fusion | bytes 16777728 | tf_op jit(solution)/shard_map/gather | solution.py:41
  20.2 7.3 %broadcast_multiply_fusion = bf16[8,16,8,4096]{3,2,1,0:T(8,128)(2,1)} fusion(bf16[8,16,8,4096]{3,2,1,0:T(8,128)(2,1)} %bitcast.71, bf16[8,16]{1,0:T(8,128)(2,1)S(1)} %convert_element_type.55), kind=kLoop, calls=%fused_computation.22 | loop fusion | flops 4194304 | bytes 16777472 | tf_op jit(solution)/shard_map/mul | solution.py:41
  27.5 7.5 %all-to-all-start = ((bf16[8,16,8,4096]{3,2,1,0:T(8,128)(2,1)}), bf16[8,16,8,4096]{3,2,1,0:T(8,128)(2,1)}, u32[]{:S(2)}, u32[]{:S(2)}) async-start(bf16[8,16,8,4096]{3,2,1,0:T(8,128)(2,1)} %broadcast_multiply_fusion), calls=%async_computation | async-start | bytes 16777216 | tf_op jit(solution)/shard_map/all_to_all | solution.py:47
  35.0 1.2 gather_fusion.5
  37.2 180.8 %all-to-all-done = bf16[8,16,8,4096]{3,2,1,0:T(8,128)(2,1)} async-done(((bf16[8,16,8,4096]{3,2,1,0:T(8,128)(2,1)}), bf16[8,16,8,4096]{3,2,1,0:T(8,128)(2,1)}, u32[]{:S(2)}, u32[]{:S(2)}) %all-to-all-start) | async-done | bytes 8388640 | tf_op jit(solution)/shard_map/all_to_all | solution.py:47
  218.1 6.5 %fusion.7 = f32[8,16,8,128]{3,2,1,0:T(8,128)} fusion(bf16[8,16,8,4096]{3,2,1,0:T(8,128)(2,1)} %all-to-all-done, bf16[128,4096]{1,0:T(8,128)(2,1)S(1)} %copy-done), kind=kOutput, calls=%fused_computation.24 | convolution fusion | flops 1073741824 | bytes 9961472 | tf_op jit(solution)/shard_map/scqd,wd->scqw/dot_general | solution.py:50
  224.6 3.6 all-to-all-start.1
  228.5 0.7 reshape.439
  229.2 37.0 %all-gather = bf16[8,4,4096]{2,1,0:T(4,128)(2,1)S(1)} all-gather(bf16[1,4,4096]{2,1,0:T(4,128)(2,1)S(1)} %bitcast.84), channel_id=1, replica_groups=mesh['vocab'=8,'token'=4] {'vocab'}, dimensions={0}, use_global_device_ids=true | all-gather | bytes 294912 | tf_op jit(solution)/shard_map/all_gather | solution.py:24
  266.2 0.8 gather_fusion.1
  267.7 3.3 all-to-all-start.4
  274.4 2.9 all-to-all-done.4
  277.4 3.3 all-to-all-start.2
  281.4 5.6 all-to-all-done.2
  287.0 3.5 all-to-all-start.3
  293.1 3.6 all-to-all-done.3
  297.6 6.8 %convolution_convert_fusion = bf16[8,16,8,4096]{3,2,1,0:T(8,128)(2,1)} fusion(bf16[128,4096]{1,0:T(8,128)(2,1)S(1)} %copy-done, f32[8,16,8,128]{3,2,1,0:T(8,128)} %fusion.7, s32[8,16,8]{2,1,0:T(8,128)S(1)} %copy.47, f32[8,16,8]{2,1,0:T(8,128)S(1)} %copy.45, f32[8,16,8]{2,1,0:T(8,128)S(1)} %copy.43), kind=kOutput, calls=%fused_computation.18 | convolution fusion | flops 1078722560 | bytes 9973760 | tf_op jit(solution)/shard_map/scqw,wd->scqd/dot_general | solution.py:86
  304.4 5.0 all-to-all-start.5
  311.1 1.1 fusion.28
  312.2 6.5 %fusion.2 = f32[128,4096]{1,0:T(8,128)} fusion(bf16[8,16,8,4096]{3,2,1,0:T(8,128)(2,1)} %all-to-all-done, f32[8,16,8,128]{3,2,1,0:T(8,128)} %fusion.7, s32[8,16,8]{2,1,0:T(8,128)S(1)} %copy.47, f32[8,16,8]{2,1,0:T(8,128)S(1)} %copy.45, f32[8,16,8]{2,1,0:T(8,128)S(1)} %copy.43), kind=kOutput, calls=%fused_computation.19 | convolution fusion | flops 1074528256 | bytes 11022336 | tf_op jit(solution)/shard_map/scqw,scqd->wd/dot_general | solution.py:92
  318.7 1.0 scatter_custom_fusion
  319.9 0.9 gather_fusion.4
  320.8 0.8 copy.51
  321.5 1.7 gather_fusion.6
  323.3 229.1 %all-reduce.3.cloned.1.call-done = f32[32,4096]{1,0:T(8,128)} async-done(((f32[32,4096]{1,0:T(8,128)}), f32[32,4096]{1,0:T(8,128)}) %all-reduce.3.cloned.1.call-update) | async-done | bytes 524304
  552.3 1.5 constant_dynamic-slice_fusion
  553.9 6.2 %gather_fusion.10 = bf16[64,8,4096]{2,1,0:T(8,128)(2,1)} fusion(bf16[128,8,4096]{2,1,0:T(8,128)(2,1)} %bitcast.20, s32[1024]{0:T(1024)S(1)} %pad_clamp_fusion.2), kind=kCustom, calls=%fused_computation.10 | custom fusion | bytes 8388864 | tf_op jit(solution)/shard_map/gather | solution.py:97
  560.0 3.2 convert_reduce_fusion
  563.7 2.2 gather_fusion.11
  (91 shorter events, 12.5 us)
Async XLA Ops:
  8.0 210.1 %copy-start = (bf16[128,4096]{1,0:T(8,128)(2,1)S(1)}, bf16[128,4096]{1,0:T(8,128)(2,1)}, u32[]{:S(2)}) copy-start(bf16[128,4096]{1,0:T(8,128)(2,1)} %param.8) | copy-start | bytes 3145732
  27.5 7.5 %copy-start.1 = (s32[128]{0:T(128)S(1)}, s32[128]{0:T(128)}, u32[]{:S(2)}) copy-start(s32[128]{0:T(128)} %param.13) | copy-start | bytes 1540
  27.5 9.7 %copy-start.3 = (s32[16,4]{0,1:T(4,128)S(1)}, s32[16,4]{0,1:T(4,128)}, u32[]{:S(2)}) copy-start(s32[16,4]{0,1:T(4,128)} %param.11) | copy-start | bytes 772
  27.5 190.6 %all-to-all-start = ((bf16[8,16,8,4096]{3,2,1,0:T(8,128)(2,1)}), bf16[8,16,8,4096]{3,2,1,0:T(8,128)(2,1)}, u32[]{:S(2)}, u32[]{:S(2)}) async-start(bf16[8,16,8,4096]{3,2,1,0:T(8,128)(2,1)} %broadcast_multiply_fusion), calls=%async_computation | async-start | bytes 16777216 | tf_op jit(solution)/shard_map/all_to_all | solution.py:47
  37.2 191.0 %copy-start.4 = (s32[8]{0:T(128)S(1)}, s32[8]{0:T(128)}, u32[]{:S(2)}) copy-start(s32[8]{0:T(128)} %param.10) | copy-start | bytes 100
  37.2 192.0 %copy-start.2 = (bf16[4,4096]{1,0:T(4,128)(2,1)S(1)}, bf16[4,4096]{1,0:T(4,128)(2,1)}, u32[]{:S(2)}) copy-start(bf16[4,4096]{1,0:T(4,128)(2,1)} %param.9) | copy-start | bytes 98308
  224.6 43.1 %all-to-all-start.1 = ((f32[8,16,8,128]{3,2,1,0:T(8,128)}), f32[8,16,8,128]{3,2,1,0:T(8,128)S(1)}, u32[]{:S(2)}, u32[]{:S(2)}) async-start(f32[8,16,8,128]{3,2,1,0:T(8,128)} %fusion.7), calls=%async_computation.1 | async-start | bytes 1048576 | tf_op jit(solution)/shard_map/all_to_all | solution.py:53
  267.7 9.7 %all-to-all-start.4 = ((s32[8,1,128]{2,1,0:T(1,128)}), s32[8,1,128]{2,1,0:T(1,128)S(1)}, u32[]{:S(2)}, u32[]{:S(2)}) async-start(s32[8,1,128]{2,1,0:T(1,128)} %reshape.439), calls=%async_computation.4 | async-start | bytes 8192 | tf_op jit(solution)/shard_map/all_to_all | solution.py:48
  277.4 9.6 %all-to-all-start.2 = ((f32[8,1,128]{2,1,0:T(1,128)}), f32[8,1,128]{2,1,0:T(1,128)S(1)}, u32[]{:S(2)}, u32[]{:S(2)}) async-start(f32[8,1,128]{2,1,0:T(1,128)} %reshape.443), calls=%async_computation.2 | async-start | bytes 8192 | tf_op jit(solution)/shard_map/all_to_all | solution.py:79
  287.0 9.6 %all-to-all-start.3 = ((f32[8,1,128]{2,1,0:T(1,128)}), f32[8,1,128]{2,1,0:T(1,128)S(1)}, u32[]{:S(2)}, u32[]{:S(2)}) async-start(f32[8,1,128]{2,1,0:T(1,128)} %reshape.441), calls=%async_computation.3 | async-start | bytes 8192 | tf_op jit(solution)/shard_map/all_to_all | solution.py:78
  304.4 249.5 %all-to-all-start.5 = ((bf16[8,16,8,4096]{3,2,1,0:T(8,128)(2,1)}), bf16[8,16,8,4096]{3,2,1,0:T(8,128)(2,1)}, u32[]{:S(2)}, u32[]{:S(2)}) async-start(bf16[8,16,8,4096]{3,2,1,0:T(8,128)(2,1)} %convolution_convert_fusion), calls=%async_computation.5 | async-start | bytes 16777216 | tf_op jit(solution)/shard_map/all_to_all | solution.py:89
  309.3 243.0 %all-reduce.3.cloned.1.call-start = ((), (), s32[]{:S(2)}) async-start(), calls=%async_computation.8 | async-start | bytes 1048576
  312.2 253.7 %reduce-scatter.2.cloned.1.call-start = ((), (), s32[]{:S(2)}) async-start(), calls=%async_computation.7 | async-start | bytes 2621440 | tf_op jit(solution)/shard_map/reduce_scatter | solution.py:91
Sparse Core Ops, SparseCore 0:
  316.9 235.4 all-reduce.2
Sparse Core Ops, SparseCore 1:
  318.8 32.6 reduce-scatter.1
where the time goes:
time: 574 us; the launch traced here: 573 us
  waiting for transfers between devices  422 us (74%)
  blocking collectives  37 us (6%)
  local copies, waits for them, and re-layouts  35.8 us (6%)
  starting transfers between devices  26.3 us (5%)
  matrix products  21.7 us (4%)
  between operations  15.9 us (3%)
  other arithmetic  14.6 us (3%)
    unnamed x3, waiting for transfers between devices  229 us
    all_to_all x1, waiting for transfers between devices, per_device(): lax.all_to_all(send_rows, 'vocab', split_axis=0, concat_axis=0, tiled=True)  181 us
    all_gather x1, blocking collectives, per_device(): panels = lax.all_gather(freq_embed, 'vocab', axis=0, tiled=True)  37 us
  transfers between devices with their start and end apart: 8, of which 5 were waited for; matrix products, arithmetic and copies ran while one was open for 7% of the time, Pallas kernels for 0%

commit v1 on v0

v1 whole, which is shorter than its diff:
```python
import jax
import jax.numpy as jnp
from jax import lax
from jax.experimental import pallas as pl
from jax.experimental.pallas import tpu as pltpu
from jax.sharding import PartitionSpec as P

D = 4096
BW = 128
K = 4
GTOK = 8
PANEL = 4
G_DEV = 16


def token_blocks(cand_blocks, group_tokens):
    where = jnp.arange(group_tokens.shape[1], dtype=jnp.int32)
    held = group_tokens[0][None, :] == where[:, None]
    group = jnp.sum(jnp.where(held, (where // GTOK)[None, :], 0), axis=1)
    group_hot = group[:, None] == jnp.arange(cand_blocks.shape[0], dtype=jnp.int32)[None, :]
    return jnp.sum(jnp.where(group_hot[:, :, None], cand_blocks[None], 0), axis=1)


def ring(hidden, cand_embed, freq_embed, owner_order, cand_blocks, group_tokens, target_slot):
    owners, shards = lax.axis_size("vocab"), lax.axis_size("token")
    me, shard = lax.axis_index("vocab"), lax.axis_index("token")
    tokens = hidden.shape[0]
    freq_count = owners * PANEL
    blocks = token_blocks(cand_blocks, group_tokens)
    turn = [(i, (i + 1) % owners) for i in range(owners)]

    def pass_on(arrays):
        return tuple(lax.ppermute(a, "vocab", turn) for a in arrays)

    def forward(step, carry):
        cand, freq, cand_scores, freq_scores = carry
        here = lax.rem(me - step + owners, owners)
        one = lax.dot_general(
            hidden, cand, (((1,), (1,)), ((), ())), preferred_element_type=jnp.float32
        )
        panel = lax.dot_general(
            hidden, freq, (((1,), (1,)), ((), ())), preferred_element_type=jnp.float32
        )
        cand_scores = jnp.where((blocks == here)[:, :, None], one[:, None, :], cand_scores)
        freq_scores = jnp.where(
            (owner_order == here)[None, :, None], panel[:, None, :], freq_scores
        )
        return pass_on((cand, freq)) + (cand_scores, freq_scores)

    cand, freq, cand_scores, freq_scores = lax.fori_loop(
        0,
        owners,
        forward,
        (
            cand_embed,
            freq_embed,
            jnp.zeros((tokens, K, BW), jnp.float32),
            jnp.zeros((tokens, owners, PANEL), jnp.float32),
        ),
    )
    scores = jnp.concatenate(
        [freq_scores.reshape(tokens, freq_count), cand_scores.reshape(tokens, K * BW)], axis=1
    )
    top = jnp.max(scores, axis=1)
    exponentials = jnp.exp(scores - top[:, None])
    total = jnp.sum(exponentials, axis=1)
    columns = jnp.arange(scores.shape[1], dtype=jnp.int32)
    hot = (target_slot[:, None] == columns[None, :]).astype(jnp.float32)
    loss = jnp.log(total) + top - jnp.sum(hot * scores, axis=1)
    prob = (exponentials * (1.0 / total)[:, None] - hot).astype(jnp.bfloat16)
    prob_freq = prob[:, :freq_count].reshape(tokens, owners, PANEL)
    prob_cand = prob[:, freq_count:].reshape(tokens, K, BW)
    zero = jnp.zeros((), jnp.bfloat16)

    def backward(step, carry):
        cand, freq, grad_cand, grad_freq, grad_hidden = carry
        here = lax.rem(me - step + owners, owners)
        one = jnp.sum(jnp.where((blocks == here)[:, :, None], prob_cand, zero), axis=1)
        panel = jnp.sum(
            jnp.where((owner_order == here)[None, :, None], prob_freq, zero), axis=1
        )
        grad_hidden = (
            grad_hidden
            + jnp.dot(one, cand, preferred_element_type=jnp.float32)
            + jnp.dot(panel, freq, preferred_element_type=jnp.float32)
        )
        grad_cand = grad_cand + lax.dot_general(
            one, hidden, (((0,), (0,)), ((), ())), preferred_element_type=jnp.float32
        )
        grad_freq = grad_freq + lax.dot_general(
            panel, hidden, (((0,), (0,)), ((), ())), preferred_element_type=jnp.float32
        )
        return pass_on((cand, freq, grad_cand, grad_freq)) + (grad_hidden,)

    _, _, grad_cand, grad_freq, grad_hidden = lax.fori_loop(
        0,
        owners,
        backward,
        (
            cand,
            freq,
            jnp.zeros(cand.shape, jnp.float32),
            jnp.zeros(freq.shape, jnp.float32),
            jnp.zeros((tokens, D), jnp.float32),
        ),
    )

    def own_rows(whole):
        rows = whole.shape[0] // shards
        return lax.dynamic_slice_in_dim(lax.psum(whole, "token"), shard * rows, rows)

    return (
        scores.astype(jnp.bfloat16),
        loss,
        grad_hidden.astype(jnp.bfloat16),
        own_rows(grad_cand),
        own_rows(grad_freq),
    )


ROWS = BW + 16
HALF = D // 2
QUART = D // 4
ZDIM = 4
YDIM = 2
OWNERS = ZDIM * YDIM
SHARDS = 4
Y, UP, DOWN, X, CORE, CORE_X, HID, PROB, PROB_X, SUM_Y, SUM_UP, SUM_DOWN, FIN = range(13)
F32 = jnp.float32
BF16 = jnp.bfloat16
NT = (((1,), (1,)), ((), ()))
TN = (((0,), (0,)), ((), ()))


def kernel(
    hid, emb, freq, blk, tgt,
    logit_out, freq_out, loss_out, gh_out, gc_out, gf_out,
    table, hq, prob, scores, part, ysend, yrecv, zsend, zrecv, fin, finr,
    send, recv, local,
):
    v = lax.axis_index("vocab")
    t = lax.axis_index("token")
    z, y = v // YDIM, v % YDIM
    x, c = t // 2, t % 2
    ynb = (v + 1 - 2 * y, t)
    xs = (v, (1 - x) * 2 + c)
    cs = (v, x * 2 + 1 - c)
    dg = (v, (1 - x) * 2 + 1 - c)

    def along(step):
        return (v + step * YDIM, t)

    def both(distance, body):
        for sign in (-1, 1):
            zz = z + sign * distance
            ok = (zz >= 0) if sign < 0 else (zz < ZDIM)
            pl.when(ok)(lambda zz=zz, sign=sign: body(zz, sign))

    barrier = pltpu.get_barrier_semaphore()

    def greet(dev):
        pl.semaphore_signal(barrier, inc=1, device_id=dev, device_id_type=pl.DeviceIdType.MESH)

    loads = [
        pltpu.make_async_copy(emb, table.at[v, pl.ds(0, BW)], local.at[0]),
        pltpu.make_async_copy(freq, table.at[v, pl.ds(BW, 16)], local.at[1]),
    ]
    for one in loads:
        one.start()
    for dev in (ynb, xs, cs, dg):
        greet(dev)
    both(1, lambda zz, sign: greet(along(sign)))
    pl.semaphore_wait(barrier, 4 + (z + ZDIM - 1) // ZDIM + (2 * ZDIM - 2 - z) // ZDIM)
    for one in loads:
        one.wait()

    def copy(src, dst, kind, slot, dev):
        return pltpu.make_async_remote_copy(
            src_ref=src, dst_ref=dst, send_sem=send.at[kind, slot], recv_sem=recv.at[kind, slot],
            device_id=dev, device_id_type=pl.DeviceIdType.MESH,
        )

    def cols(start, width):
        return pl.ds(pl.multiple_of(start, QUART), width)

    my_half = cols(c * HALF, HALF)
    other_half = cols((1 - c) * HALF, HALF)

    def quarter(xx, cc):
        return cols((cc * 2 + xx) * QUART, QUART)

    my_q = quarter(x, c)
    xs_q = quarter(1 - x, c)

    def block(kind, vb, part_of, dev):
        view = table.at[vb, :, part_of]
        return copy(view, view, kind, vb, dev)

    def zkind(sign):
        return UP if sign > 0 else DOWN

    def hid_to(dev, xx, cc):
        return pltpu.make_async_remote_copy(
            src_ref=hid.at[:, quarter(xx, cc)], dst_ref=hq.at[t],
            send_sem=send.at[HID, dev[1]], recv_sem=recv.at[HID, t],
            device_id=dev, device_id_type=pl.DeviceIdType.MESH,
        )

    def hid_from(dev):
        return pltpu.make_async_remote_copy(
            src_ref=hid.at[:, my_q], dst_ref=hq.at[dev[1]],
            send_sem=send.at[HID, dev[1]], recv_sem=recv.at[HID, dev[1]],
            device_id=dev, device_id_type=pl.DeviceIdType.MESH,
        )

    both(1, lambda zz, sign: block(zkind(sign), v, my_half, along(sign)).start())
    block(Y, v, my_half, ynb).start()
    hid_to(xs, 1 - x, c).start()
    hid_to(dg, 1 - x, 1 - c).start()
    hid_to(cs, x, 1 - c).start()
    hq[t] = hid[:, my_q]

    def score(vb):
        def step(i, total):
            at = cols(i * QUART, QUART)
            return total + lax.dot_general(
                hid[:, at], table[vb, pl.ds(0, BW), at], NT, preferred_element_type=F32
            )

        scores[vb] = lax.fori_loop(0, 4, step, jnp.zeros((BW, BW), F32))

    score(v)

    def same_y(zz):
        return zz * YDIM + y

    def other_y(zz):
        return zz * YDIM + 1 - y

    def arrive_z(distance):
        def body(zz, sign):
            vb = same_y(zz)
            got = my_half if distance == 1 else my_q
            kind = zkind(-sign)
            block(kind, vb, got, ynb).wait_recv()
            onward = z - sign
            ok = (onward < ZDIM) if sign < 0 else (onward >= 0)
            pl.when(ok)(lambda: block(kind, vb, my_q, along(-sign)).start())
            block(Y, vb, my_q, ynb).start()
            if distance > 1:
                block(X, vb, my_q, xs).start()
            block(CORE, vb, got, cs).start()

        both(distance, body)

    def arrive_y(distance):
        def body(zz, sign):
            vb = other_y(zz)
            block(Y, vb, my_q, ynb).wait_recv()
            block(X, vb, my_q, xs).start()
            block(CORE, vb, my_q, cs).start()

        both(distance, body)

    def arrive_x(distance, of):
        def body(zz, sign):
            vb = of(zz)
            block(X, vb, xs_q, xs).wait_recv()
            block(CORE_X, vb, xs_q, cs).start()

        both(distance, body)

    def finish_half(vb):
        block(CORE, vb, other_half, cs).wait_recv()
        score(vb)

    def finish(distance, of):
        def body(zz, sign):
            vb = of(zz)
            block(CORE, vb, quarter(x, 1 - c), cs).wait_recv()
            block(CORE_X, vb, quarter(1 - x, 1 - c), cs).wait_recv()
            score(vb)

        both(distance, body)

    arrive_z(1)
    arrive_z(2)
    block(Y, other_y(z), my_half, ynb).wait_recv()
    block(CORE, other_y(z), my_half, cs).start()
    arrive_y(1)
    arrive_z(3)
    arrive_x(2, same_y)
    both(1, lambda zz, sign: finish_half(same_y(zz)))
    finish_half(other_y(z))
    arrive_x(1, other_y)
    arrive_y(2)
    finish(2, same_y)
    arrive_y(3)
    arrive_x(3, same_y)
    finish(1, other_y)
    arrive_x(2, other_y)
    arrive_x(3, other_y)
    finish(3, same_y)
    finish(2, other_y)
    finish(3, other_y)

    ftab = table[:, pl.ds(BW, 16), :].reshape(OWNERS * 16, D)
    fscores = lax.dot_general(hid[...], ftab, NT, preferred_element_type=F32)
    freq_out[...] = fscores
    lane = lax.broadcasted_iota(jnp.int32, (BW, BW), 1)
    flive = lane % 16 < PANEL
    low = F32(-3.0e38)

    def chosen(vb):
        return (
            (blk[:, 0:1] == vb) | (blk[:, 1:2] == vb) | (blk[:, 2:3] == vb) | (blk[:, 3:4] == vb)
        )

    high = jnp.where(flive, fscores, low)
    for vb in range(OWNERS):
        high = jnp.maximum(high, jnp.where(chosen(vb), scores[vb], low))
    top = jnp.max(high, axis=1, keepdims=True)
    fexp = jnp.where(flive, jnp.exp(jnp.where(flive, fscores, low) - top), 0.0)
    fhot = lane == tgt[:, 2:3]
    total = fexp
    picked = jnp.where(fhot, fscores, 0.0)
    for vb in range(OWNERS):
        total = total + jnp.where(chosen(vb), jnp.exp(jnp.where(chosen(vb), scores[vb], low) - top), 0.0)
        hot = (tgt[:, 0:1] == vb) & (lane == tgt[:, 1:2])
        picked = picked + jnp.where(hot, scores[vb], 0.0)
    total = jnp.sum(total, axis=1, keepdims=True)
    inverse = 1.0 / total
    for vb in range(OWNERS):
        live = chosen(vb)
        hot = ((tgt[:, 0:1] == vb) & (lane == tgt[:, 1:2])).astype(F32)
        value = jnp.where(live, jnp.exp(jnp.where(live, scores[vb], low) - top) * inverse, 0.0)
        prob[t, :, pl.ds(vb * BW, BW)] = (value - hot).astype(BF16)
    prob[t, :, pl.ds(OWNERS * BW, BW)] = (fexp * inverse - fhot.astype(F32)).astype(BF16)

    def prob_copy(kind, of, dev):
        return copy(prob.at[of], prob.at[of], kind, of, dev)

    prob_copy(PROB, t, xs).start()
    prob_copy(PROB_X, t, cs).start()

    loss = jnp.log(total) + top - jnp.sum(picked, axis=1, keepdims=True)
    loss_out[...] = jnp.broadcast_to(loss, (BW, BW))
    for k in range(K):
        mine = jnp.zeros((BW, BW), F32)
        for vb in range(OWNERS):
            mine = jnp.where(blk[:, k : k + 1] == vb, scores[vb], mine)
        logit_out[:, pl.ds(k * BW, BW)] = mine.astype(BF16)

    prob_copy(PROB, xs[1], xs).wait_recv()
    copy(prob.at[xs[1]], prob.at[xs[1]], PROB_X, xs[1], cs).start()
    hid_from(xs).wait_recv()
    hid_from(dg).wait_recv()
    hid_from(cs).wait_recv()
    prob_copy(PROB_X, cs[1], cs).wait_recv()
    prob_copy(PROB_X, dg[1], cs).wait_recv()

    tokens = SHARDS * BW
    fpart = lax.dot_general(
        prob[:, :, pl.ds(OWNERS * BW, BW)].reshape(tokens, BW),
        hq[...].reshape(tokens, QUART), TN, preferred_element_type=F32,
    ).reshape(ZDIM, YDIM, 16, QUART)
    fkeep = jnp.where(y == 0, fpart[:, 0], fpart[:, 1])
    fgive = jnp.where(y == 0, fpart[:, 1], fpart[:, 0])
    ysend[:, pl.ds(BW, 16), :] = fgive.astype(BF16)
    part[:, pl.ds(BW, 16), :] = fkeep

    def cand_part(vb):
        at = pl.ds(pl.multiple_of(vb * BW, BW), BW)
        return lax.dot_general(
            prob[:, :, at].reshape(tokens, BW), hq[...].reshape(tokens, QUART), TN,
            preferred_element_type=F32,
        )

    def sum_y(zz):
        return copy(ysend.at[zz], yrecv.at[zz], SUM_Y, zz, ynb)

    def give(zz, sign):
        ysend[zz, pl.ds(0, BW), :] = cand_part(other_y(zz)).astype(BF16)
        sum_y(zz).start()

    def keep(zz, sign):
        part[zz, pl.ds(0, BW), :] = cand_part(same_y(zz))

    for distance in (3, 2, 1):
        both(distance, give)
    give(z, 0)
    for distance in (3, 2, 1):
        both(distance, keep)
    keep(z, 0)

    def sum_z(zz, sign):
        kind = SUM_UP if sign > 0 else SUM_DOWN
        return copy(zsend.at[zz], zrecv.at[0 if sign > 0 else 1, zz], kind, zz, along(sign))

    def pass_on(zz, sign):
        sum_y(zz).wait_recv()
        behind = (z > 0) if sign > 0 else (z < ZDIM - 1)

        @pl.when(behind)
        def _():
            sum_z(zz, sign).wait_recv()
            zsend[zz] = (
                part[zz] + yrecv[zz].astype(F32) + zrecv[0 if sign > 0 else 1, zz].astype(F32)
            ).astype(BF16)

        @pl.when(jnp.logical_not(behind))
        def _():
            zsend[zz] = (part[zz] + yrecv[zz].astype(F32)).astype(BF16)

        sum_z(zz, sign).start()

    def grad_rows(i, carry):
        at = pl.ds(pl.multiple_of(i * 512, 512), 512)
        mine = prob[t]
        total = jnp.dot(
            mine[:, : OWNERS * BW], table[:, pl.ds(0, BW), at].reshape(OWNERS * BW, 512),
            preferred_element_type=F32,
        ) + jnp.dot(
            mine[:, OWNERS * BW :], table[:, pl.ds(BW, 16), at].reshape(OWNERS * 16, 512),
            preferred_element_type=F32,
        )
        gh_out[:, at] = total.astype(BF16)
        return carry

    both(3, pass_on)
    lax.fori_loop(0, 8, grad_rows, 0)
    both(2, pass_on)
    both(1, pass_on)
    sum_y(z).wait_recv()
    part[z] = part[z] + yrecv[z].astype(F32)

    def last(zz, sign):
        sum_z(z, -sign).wait_recv()
        part[z] = part[z] + zrecv[0 if sign < 0 else 1, z].astype(F32)

    both(1, last)
    for one in range(SHARDS):
        fin[one, pl.ds(0, 32), :] = part[z, pl.ds(one * 32, 32), :].astype(BF16)
        fin[one, pl.ds(32, 16), :] = part[z, pl.ds(BW, 16), :].astype(BF16)

    def fin_to(dev):
        return pltpu.make_async_remote_copy(
            src_ref=fin.at[dev[1]], dst_ref=finr.at[t],
            send_sem=send.at[FIN, dev[1]], recv_sem=recv.at[FIN, t],
            device_id=dev, device_id_type=pl.DeviceIdType.MESH,
        )

    def fin_from(dev):
        return pltpu.make_async_remote_copy(
            src_ref=fin.at[dev[1]], dst_ref=finr.at[dev[1]],
            send_sem=send.at[FIN, dev[1]], recv_sem=recv.at[FIN, dev[1]],
            device_id=dev, device_id_type=pl.DeviceIdType.MESH,
        )

    for dev in (xs, dg, cs):
        fin_to(dev).start()
    finr[t] = fin[t]

    both(1, lambda zz, sign: block(zkind(sign), v, my_half, along(sign)).wait_send())
    block(Y, v, my_half, ynb).wait_send()
    for dev in (xs, dg, cs):
        hid_to(dev, x, c).wait_send()
    block(CORE, other_y(z), my_half, cs).wait_send()
    for distance in (1, 2, 3):

        def sent(zz, sign, distance=distance):
            vb = same_y(zz)
            got = my_half if distance == 1 else my_q
            kind = zkind(-sign)
            onward = z - sign
            ok = (onward < ZDIM) if sign < 0 else (onward >= 0)
            pl.when(ok)(lambda: block(kind, vb, my_q, along(-sign)).wait_send())
            block(Y, vb, my_q, ynb).wait_send()
            block(CORE, vb, got, cs).wait_send()
            if distance > 1:
                block(X, vb, my_q, xs).wait_send()
                block(CORE_X, vb, xs_q, cs).wait_send()
            block(X, other_y(zz), my_q, xs).wait_send()
            block(CORE, other_y(zz), my_q, cs).wait_send()
            block(CORE_X, other_y(zz), xs_q, cs).wait_send()
            sum_y(zz).wait_send()
            sum_z(zz, sign).wait_send()

        both(distance, sent)
    sum_y(z).wait_send()
    prob_copy(PROB, t, xs).wait_send()
    prob_copy(PROB_X, t, cs).wait_send()
    prob_copy(PROB_X, xs[1], cs).wait_send()
    for dev in (xs, dg, cs):
        fin_to(dev).wait_send()
        fin_from(dev).wait_recv()

    row = lax.broadcasted_iota(jnp.int32, (16, QUART), 0)
    for one in range(SHARDS):
        place = (one % 2) * 2 + one // 2
        at = pl.ds(place * QUART, QUART)
        gc_out[:, at] = finr[one, pl.ds(0, 32), :].astype(F32)
        gf_out[:, at] = jnp.sum(
            jnp.where(row == t, finr[one, pl.ds(32, 16), :].astype(F32), 0.0), axis=0, keepdims=True
        )


def dense(hidden, cand_embed, freq_embed, owner_order, cand_blocks, group_tokens, target_slot):
    tokens = hidden.shape[0]
    freq_count = OWNERS * PANEL
    blocks = token_blocks(cand_blocks, group_tokens)
    in_cand = target_slot >= freq_count
    column = jnp.where(in_cand, target_slot - freq_count, 0)
    rank_hot = (column // BW)[:, None] == jnp.arange(K, dtype=jnp.int32)[None, :]
    target_block = jnp.where(in_cand, jnp.sum(jnp.where(rank_hot, blocks, 0), axis=1), -1)
    word = jnp.where(in_cand, column % BW, -1)
    slot = jnp.where(in_cand, 0, target_slot)
    panel_hot = (slot // PANEL)[:, None] == jnp.arange(OWNERS, dtype=jnp.int32)[None, :]
    panel = jnp.sum(jnp.where(panel_hot, owner_order[None, :], 0), axis=1)
    freq_lane = jnp.where(in_cand, -1, panel * 16 + slot % PANEL)
    tgt = jnp.stack([target_block, word, freq_lane, freq_lane], axis=1)
    freq_pad = jnp.pad(freq_embed, ((0, 16 - PANEL), (0, 0)))
    vmem = pl.BlockSpec(memory_space=pltpu.VMEM)
    hbm = pl.BlockSpec(memory_space=pl.ANY)
    shape = jax.ShapeDtypeStruct
    logits, freq_scores, loss, grad_hidden, grad_cand, grad_freq = pl.pallas_call(
        kernel,
        out_shape=(
            shape((tokens, K * BW), BF16),
            shape((tokens, BW), F32),
            shape((tokens, BW), F32),
            shape((tokens, D), BF16),
            shape((BW // SHARDS, D), F32),
            shape((1, D), F32),
        ),
        in_specs=[vmem, hbm, hbm, vmem, vmem],
        out_specs=(vmem,) * 6,
        scratch_shapes=[
            pltpu.VMEM((OWNERS, ROWS, D), BF16),
            pltpu.VMEM((SHARDS, BW, QUART), BF16),
            pltpu.VMEM((SHARDS, BW, OWNERS * BW + BW), BF16),
            pltpu.VMEM((OWNERS, BW, BW), F32),
            pltpu.VMEM((ZDIM, ROWS, QUART), F32),
            pltpu.VMEM((ZDIM, ROWS, QUART), BF16),
            pltpu.VMEM((ZDIM, ROWS, QUART), BF16),
            pltpu.VMEM((ZDIM, ROWS, QUART), BF16),
            pltpu.VMEM((2, ZDIM, ROWS, QUART), BF16),
            pltpu.VMEM((SHARDS, 48, QUART), BF16),
            pltpu.VMEM((SHARDS, 48, QUART), BF16),
            pltpu.SemaphoreType.DMA((13, OWNERS)),
            pltpu.SemaphoreType.DMA((13, OWNERS)),
            pltpu.SemaphoreType.DMA((2,)),
        ],
        compiler_params=pltpu.CompilerParams(
            collective_id=0, has_side_effects=True, vmem_limit_bytes=56 << 20
        ),
    )(hidden, cand_embed, freq_pad, blocks, tgt)
    panels = freq_scores.reshape(tokens, OWNERS, 16)[:, :, :PANEL]
    order_hot = owner_order[:, None] == jnp.arange(OWNERS, dtype=jnp.int32)[None, :]
    ordered = jnp.sum(
        jnp.where(order_hot[None, :, :, None], panels[:, None], 0.0), axis=2
    ).reshape(tokens, freq_count)
    all_logits = jnp.concatenate([ordered.astype(BF16), logits], axis=1)
    return (all_logits, loss[:, 0], grad_hidden, grad_cand, grad_freq)


def per_device(hidden, *rest):
    fits = (lax.axis_size("vocab"), lax.axis_size("token")) == (OWNERS, SHARDS)
    fits = fits and hidden.shape[0] == BW
    return (dense if fits else ring)(hidden, *rest)


def solution(mesh):
    in_specs = (
        P(("vocab", "token"), None),
        P("vocab", None),
        P("vocab", None),
        P(),
        P(("vocab", "token"), None),
        P(("vocab", "token"), None),
        P(("vocab", "token")),
    )
    out_specs = (
        P(("vocab", "token"), None),
        P(("vocab", "token")),
        P(("vocab", "token"), None),
        P(("vocab", "token"), None),
        P(("vocab", "token"), None),
    )
    return jax.shard_map(
        per_device, mesh=mesh, in_specs=in_specs, out_specs=out_specs, check_vma=False
    )
```

time: 574 us -> 128 us (0.22)
  waiting for transfers between devices: 422 us -> 0 us
  Pallas kernels: 0 us -> 115 us
  blocking collectives: 37 us -> 0 us
  starting transfers between devices: 26.3 us -> 0 us
  local copies, waits for them, and re-layouts: 35.8 us -> 10.8 us
  matrix products: 21.7 us -> 0 us
  between operations: 15.9 us -> 0.74 us
  other arithmetic: 14.6 us -> 0.65 us
    unnamed x3 -> x0, waiting for transfers between devices: 229 us -> none
    all_to_all x6 -> x0, waiting for transfers between devices: 193 us -> none  [the longest x1 181 us: per_device(): lax.all_to_all(send_rows, 'vocab', split_axis=0, concat_axis=0, tiled=True)]
    pallas_call x0 -> x1, Pallas kernels: none -> 115 us  [dense(): pl.pallas_call(kernel, out_shape=(shape((tokens, K * BW), BF16), shape((t...]
    all_gather x1 -> x0, blocking collectives: 37 us -> none  [per_device(): panels = lax.all_gather(freq_embed, 'vocab', axis=0, tiled=True)]
    gather x15 -> x0, local copies, waits for them, and re-layouts: 26.3 us -> none  [the longest x1 6.43 us: per_device(): group_rows[group_of] * slot_mask]
    all_to_all x6 -> x0, starting transfers between devices: 26.2 us -> none  [the longest x1 7.46 us: per_device(): lax.all_to_all(send_rows, 'vocab', split_axis=0, concat_axis=0, tiled=True)]
    dot_general x6 -> x0, matrix products: 21.7 us -> none  [the longest x1 6.79 us: per_device(): jnp.einsum('scqw,wd->scqd', prob_here, cand_embed, preferred_element_type...]
    mul x5 -> x0, other arithmetic: 7.29 us -> none  [the longest x1 7.27 us: per_device(): group_rows[group_of] * slot_mask]
  transfers between devices with their start and end apart: 8 -> 0, of which waited for: 5 -> 0; matrix products, arithmetic and copies ran while one was open for 7% -> 0% of each run, Pallas kernels for 0% -> 0%
where the time goes in v1:
time: 128 us
  Pallas kernels  115 us (90%)
  local copies, waits for them, and re-layouts  10.8 us (8%)
    pallas_call x1, Pallas kernels, dense(): pl.pallas_call(kernel, out_shape=(shape((tokens, K * BW), BF16), shape((t...  115 us
    unnamed x22, local copies, waits for them, and re-layouts  6.9 us

profile of v1, /device:TPU:0, one launch (start us, length us, event | category | flops | bytes accessed | tf_op | source)
XLA Modules:
  0.0 127.5 jit_solution(3164310158674221369)
XLA Ops:
  0.6 0.0 copy-start.7
  0.7 0.6 copy-done.7
  1.3 0.0 copy-start.8
  1.3 0.1 select_reduce_fusion.1
  1.4 0.5 copy-done.8
  1.9 0.0 copy-start.5
  1.9 0.1 iota_compare_fusion.3
  2.0 0.6 copy-done.5
  2.6 0.0 copy-start.6
  2.6 0.1 select_reduce_fusion.2
  2.7 0.6 copy-done.6
  3.3 0.1 select_reduce_fusion.3
  3.4 0.7 copy.34.tgt
  4.2 0.7 copy.33.blk
  4.9 0.0 copy-done.3
  4.9 0.7 pad.4.freq
  5.6 115.4 %shard_map.110 = (bf16[128,512]{1,0:T(8,128)(2,1)}, f32[128,128]{1,0:T(8,128)}, f32[128,128]{1,0:T(8,128)}, bf16[128,4096]{1,0:T(8,128)(2,1)}, f32[32,4096]{1,0:T(8,128)}, /*index=5*/f32[1,4096]{1,0:T(1,128)}) custom-call(bf16[128,4096]{1,0:T(8,128)(2,1)} %hid.1, bf16[128,4096]{1,0:T(8,128)(2,1)} %emb.1, bf16[16,4096]{1,0:T(8,128)(2,1)} %pad.4.freq, ...), custom_call_target="tpu_custom_call" | custom-call | tf_op jit(solution)/shard_map/pallas_call | solution.py:526
  121.0 0.0 copy-start.2
  121.0 1.0 copy.35
  122.0 0.0 copy-start.1
  122.0 0.1 select_reduce_fusion
  122.1 0.0 copy-done.2
  122.1 0.6 slice_reduce_fusion
  122.8 0.1 copy.37
  122.9 0.0 copy-done.1
  122.9 0.1 pad_maximum_fusion
  123.0 0.8 copy.38
  123.8 2.3 %copy.42 = bf16[128,4096]{1,0:T(8,128)(2,1)} copy(bf16[128,4096]{1,0:T(8,128)(2,1)} %get-tuple-element.50) | data formatting | bytes 2097152
  126.1 0.0 copy-done
  126.1 0.8 copy.43
  126.9 0.0 copy-done.4
  126.9 0.6 copy.44
  (11 shorter events, 0.1 us)
Async XLA Ops:
  0.6 0.7 copy-start.7
  1.3 0.7 copy-start.8
  1.9 0.7 copy-start.5
  2.6 0.7 copy-start.6
  4.2 0.8 copy-start.3
  121.0 1.1 copy-start.2
  122.0 0.9 copy-start.1
  123.8 2.3 %copy-start = (f32[32,4096]{1,0:T(8,128)S(1)}, f32[32,4096]{1,0:T(8,128)}, u32[]{:S(2)}) copy-start(f32[32,4096]{1,0:T(8,128)} %get-tuple-element.51) | copy-start | bytes 1572868
  126.1 0.8 copy-start.4
